TPU v7x, 512 devices: a whole 4x4x16 slice. The times are simulated.
512 devices in a mesh: enc: 16 (over x, z_hi), seq: 8 (over y, core), tp: 4 (over z_lo).
Axes of the slice: x: 4, y: 4, z: 16 (z_hi: 4, z_lo: 4; z = z_hi * 4 + z_lo), core: 2. Of those that a mesh axis runs over, the one named last changes fastest.
Arguments:
- visual_key_value: bfloat16 [16, 16, 256, 2048], P(None, 'seq', 'enc', 'tp'), may hold values from -4.5 to 4.5
- patch_blocks: int32 [16, 16], P('enc'), may hold values from 1 to 8
- queries: bfloat16 [16, 16, 32, 8192], P('enc', 'seq', None, 'tp'), may hold values from -113 to 113
- suffix_key_value: bfloat16 [16, 16, 32, 2048], P('enc', 'seq', None, 'tp'), may hold values from -6 to 6
- suffix_hidden_state: bfloat16 [16, 16, 32, 8192], P('enc', 'seq', None, 'tp'), may hold values from -6 to 6
- down_weight: bfloat16 [8192, 128], P('tp'), may hold values from -0.0625 to 0.0625
- up_weight: bfloat16 [128, 8192], P(None, 'tp'), may hold values from -1.5 to 1.5
- question_adapter: int32 [16, 16], P('enc', 'seq'), may hold values from 0 to 7
- suffix_token_length: int32 [16, 16], P('enc', 'seq'), may hold values from 1 to 32
Outputs:
- context: bfloat16 [16, 16, 32, 8192], P('enc', 'seq', None, 'tp')
All inputs are finite; a program needn't handle non-finite values.
Results may differ from a plain program's by a relative error of at most 0.0087.
Values may be sent and summed in bfloat16 or wider, within the bound.
A program may use at most 64 MiB of HBM per device.

v0:
```python
import math
import jax
import jax.numpy as jnp
from jax import lax
from jax.sharding import PartitionSpec as P

HEAD_SIZE = 128
ADAPTER_RANK = 16
NEG_BIG = -1e30
ADAPTER_SCALE = 2.0


def sent_to_all(shard, axis):
    copies = jnp.broadcast_to(shard, (lax.axis_size(axis), *shard.shape))
    return lax.all_to_all(copies, axis, split_axis=0, concat_axis=0, tiled=True)


def over_copies(shard, axis):
    return sent_to_all(shard, axis).sum(axis=0)


def per_device(
    visual_key_value,
    patch_blocks,
    queries,
    suffix_key_value,
    suffix_hidden_state,
    down_weight,
    up_weight,
    question_adapter,
    suffix_token_length,
):
    docs_here, asked_here, suffix_len, query_feature_width = queries.shape
    kv_local = suffix_key_value.shape[3] // (2 * HEAD_SIZE)
    head_group = query_feature_width // (kv_local * HEAD_SIZE)
    asked_rows = asked_here * suffix_len
    row_totals = docs_here * asked_rows
    inverse = 1.0 / math.sqrt(HEAD_SIZE)
    enc_count = lax.axis_size("enc")
    hidden_state_rows = suffix_hidden_state.reshape(row_totals, suffix_hidden_state.shape[3])
    reduced_features = jnp.dot(hidden_state_rows, down_weight, preferred_element_type=jnp.float32)
    owning_question = lax.broadcasted_iota(jnp.int32, (1, down_weight.shape[1]), 1) // ADAPTER_RANK
    row_ids = jnp.broadcast_to(
        question_adapter[:, :, None], (docs_here, asked_here, suffix_len)
    ).reshape(row_totals, 1)
    reduced_features = jnp.where(owning_question == row_ids, reduced_features, 0.0)
    selected_adapter = over_copies(reduced_features, "tp").astype(jnp.bfloat16)
    raised_features = jnp.dot(selected_adapter, up_weight, preferred_element_type=jnp.float32)
    query_matrix = (
        queries.reshape(row_totals, query_feature_width).astype(jnp.float32)
        + ADAPTER_SCALE * raised_features
    ).astype(jnp.bfloat16)
    query_matrix = query_matrix.reshape(docs_here, asked_rows, kv_local, head_group, HEAD_SIZE)
    suffix_pairs = suffix_key_value.reshape(
        docs_here, asked_here, suffix_len, kv_local, 2, HEAD_SIZE
    )
    query_split = query_matrix.reshape(
        docs_here, asked_here, suffix_len, kv_local, head_group, HEAD_SIZE
    )
    suffix_scores = (
        jnp.einsum(
            "bqikgd,bqjkd->bkgqij",
            query_split,
            suffix_pairs[:, :, :, :, 0, :],
            preferred_element_type=jnp.float32,
        )
        * inverse
    )
    positions = lax.broadcasted_iota(jnp.int32, (suffix_len, suffix_len), 0)
    columns = lax.broadcasted_iota(jnp.int32, (suffix_len, suffix_len), 1)
    causal = columns <= positions
    within = (
        lax.broadcasted_iota(jnp.int32, (1, 1, suffix_len), 2) < suffix_token_length[:, :, None]
    )
    suffix_mask = (causal[None, None, :, :] & within[:, :, None, :])[:, None, None]
    suffix_scores = jnp.where(suffix_mask, suffix_scores, NEG_BIG)
    suffix_peak = suffix_scores.max(axis=-1)
    suffix_weights = jnp.where(suffix_mask, jnp.exp(suffix_scores - suffix_peak[..., None]), 0.0)
    running = suffix_peak.reshape(docs_here, kv_local, head_group, asked_rows)
    totals = suffix_weights.sum(axis=-1).reshape(docs_here, kv_local, head_group, asked_rows)
    numerators = jnp.einsum(
        "bkgqij,bqjkd->bkgqid",
        suffix_weights.astype(jnp.bfloat16),
        suffix_pairs[:, :, :, :, 1, :],
        preferred_element_type=jnp.float32,
    )
    numerators = numerators.reshape(docs_here, kv_local, head_group, asked_rows, HEAD_SIZE)
    carried = (running, totals, numerators)
    exchanged = lax.all_to_all(visual_key_value, "enc", split_axis=0, concat_axis=0, tiled=True)
    key_piece = lax.all_gather(exchanged, "seq", axis=1, tiled=True)
    peaks_now, totals_now, numer_now = carried
    tile_rows, page_count, tile_len, piece_width = key_piece.shape
    key_values = key_piece.reshape(enc_count, docs_here, page_count, tile_len, piece_width)
    key_values = jnp.moveaxis(key_values, 1, 0).reshape(
        docs_here, enc_count * page_count * tile_len, kv_local, 2, HEAD_SIZE
    )
    token_pos = lax.broadcasted_iota(
        jnp.int32, (1, enc_count, 1, tile_len), 1
    ) * tile_len + lax.broadcasted_iota(jnp.int32, (1, enc_count, 1, tile_len), 3)
    live_keys = 8 * token_pos < patch_blocks[:, None, :, None] * (enc_count * tile_len)
    live_keys = live_keys.reshape(docs_here, 1, 1, 1, enc_count * page_count * tile_len)
    scores = (
        jnp.einsum(
            "bnkgd,blkd->bkgnl",
            query_matrix,
            key_values[:, :, :, 0, :],
            preferred_element_type=jnp.float32,
        )
        * inverse
    )
    scores = jnp.where(live_keys, scores, NEG_BIG)
    updated = jnp.maximum(peaks_now, scores.max(axis=-1))
    rescale = jnp.exp(peaks_now - updated)
    weights = jnp.where(live_keys, jnp.exp(scores - updated[..., None]), 0.0)
    totals_next = totals_now * rescale + weights.sum(axis=-1)
    numer_next = numer_now * rescale[..., None] + jnp.einsum(
        "bkgnl,blkd->bkgnd",
        weights.astype(jnp.bfloat16),
        key_values[:, :, :, 1, :],
        preferred_element_type=jnp.float32,
    )
    carried = (updated, totals_next, numer_next)
    running, totals, numerators = carried
    context = numerators / totals[..., None]
    context = jnp.transpose(context, (0, 3, 1, 2, 4)).reshape(
        docs_here, asked_here, suffix_len, query_feature_width
    )
    kept_rows = (
        lax.broadcasted_iota(jnp.int32, (1, 1, suffix_len), 2) < suffix_token_length[:, :, None]
    )
    return jnp.where(kept_rows[:, :, :, None], context, 0.0).astype(jnp.bfloat16)


def solution(mesh):
    placed = (
        P(None, "seq", "enc", "tp"),
        P("enc", None),
        P("enc", "seq", None, "tp"),
        P("enc", "seq", None, "tp"),
        P("enc", "seq", None, "tp"),
        P("tp", None),
        P(None, "tp"),
        P("enc", "seq"),
        P("enc", "seq"),
    )
    return jax.shard_map(
        per_device,
        mesh=mesh,
        in_specs=placed,
        out_specs=P("enc", "seq", None, "tp"),
        check_vma=False,
    )
```

profile of v0, /device:TPU:1, one launch (start us, length us, event | category | flops | bytes accessed | tf_op | source)
XLA Modules:
  0.0 128.2 jit_solution(13732557373285925791)
XLA Ops:
  6.5 0.0 copy-start
  6.5 0.0 all-gather.2.cloned.1.call-start
  6.5 45.5 %all_to_all.10 = bf16[16,2,16,512]{3,2,1,0:T(8,128)(2,1)} all-to-all(bf16[16,2,16,512]{3,2,1,0:T(8,128)(2,1)} %param.9), channel_id=1, replica_groups=mesh['enc'=16,'seq'=8,'tp'=4] {'enc'}, dimensions={0} | all-to-all | bytes 1048576 | tf_op jit(solution)/shard_map/all_to_all | solution.py:89
  52.1 0.0 all-gather.2.cloned.1.call-update
  52.1 0.7 broadcast_in_dim.81
  52.8 0.1 broadcast_in_dim.82
  52.9 1.3 %convolution_select_fusion = f32[64,128]{1,0:T(8,128)S(1)} fusion(bf16[64,2048]{1,0:T(8,128)(2,1)} %bitcast.147, bf16[2048,128]{1,0:T(8,128)(2,1)} %param.14, s32[128]{0:T(128)S(1)} %and_select_fusion, s32[64]{0:T(128)S(1)} %broadcast_in_dim.82), kind=kOutput, calls=%fused_computation.24 | convolution fusion | flops 33570816 | bytes 819968 | tf_op jit(solution)/shard_map/dot_general | solution.py:41
  54.3 0.7 broadcast_in_dim.84
  54.9 9.1 %all-to-all-start = ((f32[4,64,128]{2,1,0:T(8,128)}), f32[4,64,128]{2,1,0:T(8,128)S(1)}, u32[]{:S(2)}, u32[]{:S(2)}) async-start(f32[4,64,128]{2,1,0:T(8,128)} %broadcast_in_dim.84), calls=%async_computation | async-start | bytes 262144 | tf_op jit(solution)/shard_map/all_to_all | solution.py:15
  64.0 0.7 multiply_bitcast_fusion
  64.7 0.1 add_multiply_fusion
  64.8 0.1 broadcast_compare_fusion
  64.9 0.1 lt.61
  65.0 0.9 reshape.308
  65.9 0.7 iota_compare_fusion.1
  66.6 0.1 fusion.39
  66.7 2.1 %all-to-all-done = f32[4,64,128]{2,1,0:T(8,128)S(1)} async-done(((f32[4,64,128]{2,1,0:T(8,128)}), f32[4,64,128]{2,1,0:T(8,128)S(1)}, u32[]{:S(2)}, u32[]{:S(2)}) %all-to-all-start) | async-done | bytes 131104 | tf_op jit(solution)/shard_map/all_to_all | solution.py:15
  68.8 0.0 copy-done
  68.8 1.2 fusion.17
  70.1 0.4 fusion.40
  70.4 0.4 fusion.25
  70.8 0.2 convolution_bitcast_fusion
  71.1 19.3 %all-gather.2.cloned.1.call-done = bf16[16,16,16,512]{3,2,1,0:T(8,128)(2,1)} async-done(((bf16[16,2,16,512]{3,2,1,0:T(8,128)(2,1)}), bf16[16,16,16,512]{3,2,1,0:T(8,128)(2,1)}) %all-gather.2.cloned.1.call-update) | async-done | bytes 4194320 | tf_op jit(solution)/shard_map/all_gather | solution.py:90
  90.3 6.9 %reshape_transpose_reshape.3 = bf16[1,4096,2,2,128]{4,3,2,1,0:T(2,128)(2,1)} reshape(bf16[16,16,16,512]{3,2,1,0:T(8,128)(2,1)} %all-gather.2.cloned.1.call-done) | data formatting | bytes 8388608 | tf_op jit(solution)/shard_map/reshape;transpose;reshape | solution.py:94
  97.2 9.0 %fusion.38 = (bf16[1,4096,2,1,128]{4,3,2,1,0:T(2,128)(2,1)S(1)}, bf16[1,4096,2,1,128]{4,3,2,1,0:T(2,128)(2,1)S(1)}) fusion(bf16[1,4096,2,2,128]{4,3,2,1,0:T(2,128)(2,1)} %reshape_transpose_reshape.3), kind=kLoop, calls=%fused_computation.56 | loop fusion | bytes 8388608 | tf_op jit(solution)/shard_map/slice | solution.py:106
  106.2 2.9 %fusion.1 = (f32[2,8,64]{1,2,0:T(8,128)S(1)}, f32[2,64,8,4096]{3,2,1,0:T(8,128)S(1)}) fusion(pred[4096]{0:T(1024)(128)(4,1)S(1)} %lt.61, bf16[1,4096,2,1,128]{4,3,2,1,0:T(2,128)(2,1)S(1)} %get-tuple-element.7, bf16[64,2,8,128]{3,2,1,0:T(8,128)(2,1)S(1)} %bitcast.143), kind=kOutput, calls=%fused_computation.3 | convolution fusion | flops 1086323712 | bytes 19144704 | tf_op jit(solution)/shard_map/bnkgd,blkd->bkgnl/dot_general | solution.py:103
  109.2 4.9 %fusion.2 = f32[2,8,64]{1,2,0:T(8,128)S(1)} fusion(f32[2,64,8,4096]{3,2,1,0:T(8,128)S(1)} %get-tuple-element.16, f32[2,8,64]{1,2,0:T(8,128)S(1)} %max.17, pred[4096]{0:T(1024)(128)(4,1)S(1)} %lt.61), kind=kLoop, calls=%fused_computation.4 | loop fusion | flops 20970496 | bytes 16789504 | tf_op jit(solution)/shard_map/reduce_sum | solution.py:115
  114.1 4.8 %fusion.21 = f32[1,64,2,8,128]{4,3,1,2,0:T(8,128)} fusion(bf16[1,4096,2,1,128]{4,3,2,1,0:T(2,128)(2,1)S(1)} %get-tuple-element.8, f32[2,64,8,4096]{3,2,1,0:T(8,128)S(1)} %get-tuple-element.16, f32[2,8,64]{1,2,0:T(8,128)S(1)} %max.17, pred[4096]{0:T(1024)(128)(4,1)S(1)} %lt.61, f32[2,8,64,128]{3,2,1,0:T(8,128)S(1)} %bitcast.146, ...), kind=kOutput, calls=%fused_computation.23 | convolution fusion | flops 1095106560 | bytes 19939328 | tf_op jit(solution)/shard_map/bkgnl,blkd->bkgnd/dot_general | solution.py:116
  118.9 1.1 copy.38
  120.0 0.5 fusion.24
  120.5 0.9 copy.39
  (9 shorter events, 0.1 us)
Async XLA Ops:
  6.5 62.3 %copy-start = (bf16[128,2048]{1,0:T(8,128)(2,1)S(1)}, bf16[128,2048]{1,0:T(8,128)(2,1)}, u32[]{:S(2)}) copy-start(bf16[128,2048]{1,0:T(8,128)(2,1)} %param.15) | copy-start | bytes 1572868
  6.5 83.8 %all-gather.2.cloned.1.call-start = ((), (), s32[]{:S(2)}) async-start(), calls=%async_computation.2 | async-start | bytes 4718592 | tf_op jit(solution)/shard_map/all_gather | solution.py:90
  54.9 13.9 %all-to-all-start = ((f32[4,64,128]{2,1,0:T(8,128)}), f32[4,64,128]{2,1,0:T(8,128)S(1)}, u32[]{:S(2)}, u32[]{:S(2)}) async-start(f32[4,64,128]{2,1,0:T(8,128)} %broadcast_in_dim.84), calls=%async_computation | async-start | bytes 262144 | tf_op jit(solution)/shard_map/all_to_all | solution.py:15
Sparse Core Ops, SparseCore 0:
  52.2 38.0 all-gather.1
where the time goes:
time: 129 us; the launch traced here: 128 us
  blocking collectives  45.5 us (35%)
  waiting for transfers between devices  21.4 us (17%)
  local copies, waits for them, and re-layouts  20.4 us (16%)
  between operations  13.5 us (10%)
  matrix products  10.8 us (8%)
  starting transfers between devices  9.1 us (7%)
  other arithmetic  7.44 us (6%)
    all_to_all x1, blocking collectives, per_device(): lax.all_to_all(visual_key_value, 'enc', split_axis=0, concat_axis=0, tile...  45.5 us
    all_gather x1, waiting for transfers between devices, per_device(): key_piece = lax.all_gather(exchanged, 'seq', axis=1, tiled=True)  19.3 us
    all_to_all x1, starting transfers between devices, sent_to_all(): return lax.all_to_all(copies, axis, split_axis=0, concat_axis=0, tiled=True)  9.1 us
    slice x1, local copies, waits for them, and re-layouts, per_device(): key_values[:, :, :, 0, :]  8.97 us
    another operation x1, local copies, waits for them, and re-layouts, per_device(): jnp.moveaxis(key_values, 1, 0)  6.92 us
    reduce_sum x1, other arithmetic, per_device(): totals_next = totals_now * rescale + weights.sum(axis=-1)  4.91 us
    dot_general x1, matrix products, per_device(): jnp.einsum('bkgnl,blkd->bkgnd', weights.astype(jnp.bfloat16), key_values[...  4.77 us
    dot_general x1, matrix products, per_device(): jnp.einsum('bnkgd,blkd->bkgnl', query_matrix, key_values[:, :, :, 0, :],...  2.92 us
  transfers between devices with their start and end apart: 2, of which 2 were waited for; matrix products, arithmetic and copies ran while one was open for 6% of the time, Pallas kernels for 0%

commit v1 on v0

--- a/solution.py
+++ b/solution.py
@@ -8,6 +8,13 @@
 ADAPTER_RANK = 16
 NEG_BIG = -1e30
 ADAPTER_SCALE = 2.0
+
+
+def swapped_in(x, axis, dim):
+    count = lax.axis_size(axis)
+    blocks = jnp.stack([x for _ in range(count)])
+    blocks = lax.all_to_all(blocks, axis, split_axis=0, concat_axis=0)
+    return jnp.concatenate(blocks, axis=dim)
 
 
 def sent_to_all(shard, axis):
@@ -87,7 +94,7 @@
     numerators = numerators.reshape(docs_here, kv_local, head_group, asked_rows, HEAD_SIZE)
     carried = (running, totals, numerators)
     exchanged = lax.all_to_all(visual_key_value, "enc", split_axis=0, concat_axis=0, tiled=True)
-    key_piece = lax.all_gather(exchanged, "seq", axis=1, tiled=True)
+    key_piece = swapped_in(exchanged, "seq", 1)
     peaks_now, totals_now, numer_now = carried
     tile_rows, page_count, tile_len, piece_width = key_piece.shape
     key_values = key_piece.reshape(enc_count, docs_here, page_count, tile_len, piece_width)

time: 129 us -> 155 us (1.20)
  the two profiles are of different devices: /device:TPU:1 before, /device:TPU:32 now
where the time goes in v1:
time: 155 us; the launch traced here: 154 us
  blocking collectives  59.3 us (38%)
  waiting for transfers between devices  44.8 us (29%)
  local copies, waits for them, and re-layouts  27.3 us (18%)
  matrix products  10.8 us (7%)
  other arithmetic  7.44 us (5%)
  starting transfers between devices  4.54 us (3%)
    all_to_all x1, blocking collectives, per_device(): lax.all_to_all(visual_key_value, 'enc', split_axis=0, concat_axis=0, tile...  46.2 us
    all_to_all x1, waiting for transfers between devices, swapped_in(): blocks = lax.all_to_all(blocks, axis, split_axis=0, concat_axis=0)  44.8 us
    all_to_all x1, blocking collectives, sent_to_all(): return lax.all_to_all(copies, axis, split_axis=0, concat_axis=0, tiled=True)  13 us
    slice x1, local copies, waits for them, and re-layouts, per_device(): key_values[:, :, :, 0, :]  8.9 us
    another operation x1, local copies, waits for them, and re-layouts, per_device(): jnp.moveaxis(key_values, 1, 0)  6.93 us
    reshape x1, local copies, waits for them, and re-layouts, swapped_in(): return jnp.concatenate(blocks, axis=dim)  5 us
    reduce_sum x1, other arithmetic, per_device(): totals_next = totals_now * rescale + weights.sum(axis=-1)  4.91 us
    dot_general x1, matrix products, per_device(): jnp.einsum('bkgnl,blkd->bkgnd', weights.astype(jnp.bfloat16), key_values[...  4.77 us
  transfers between devices with their start and end apart: 1, of which 1 were waited for; matrix products, arithmetic and copies ran while one was open for 3% of the time, Pallas kernels for 0%

profile of v1, /device:TPU:32, one launch (start us, length us, event | category | flops | bytes accessed | tf_op | source)
XLA Modules:
  0.0 154.2 jit_solution(2684932294754566327)
XLA Ops:
  0.0 0.0 copy-start
  0.0 0.8 broadcast_in_dim.81
  0.8 0.1 broadcast_in_dim.82
  0.9 1.3 convolution_select_fusion
  2.2 13.0 %all_to_all.15 = f32[4,64,128]{2,1,0:T(8,128)S(1)} all-to-all(f32[4,64,128]{2,1,0:T(8,128)S(1)} %broadcast_in_dim.84), channel_id=1, replica_groups=mesh['enc'=16,'seq'=8,'tp'=4] {'tp'}, dimensions={0} | all-to-all | bytes 262144 | tf_op jit(solution)/shard_map/all_to_all | solution.py:22
  15.3 46.2 %all_to_all.16 = bf16[16,2,16,512]{3,2,1,0:T(8,128)(2,1)S(1)} all-to-all(bf16[16,2,16,512]{3,2,1,0:T(8,128)(2,1)} %param.9), channel_id=1, replica_groups=mesh['enc'=16,'seq'=8,'tp'=4] {'enc'}, dimensions={0} | all-to-all | bytes 1048576 | tf_op jit(solution)/shard_map/all_to_all | solution.py:96
  61.5 2.5 %stack.2 = bf16[8,16,2,16,512]{4,3,2,1,0:T(8,128)(2,1)} broadcast(bf16[16,2,16,512]{3,2,1,0:T(8,128)(2,1)S(1)} %all_to_all.16), dimensions={1,2,3,4} | broadcast | bytes 4718592 | tf_op jit(solution)/shard_map/stack | solution.py:15
  64.0 4.5 %all-to-all-start.2 = ((bf16[8,16,2,16,512]{4,3,2,1,0:T(8,128)(2,1)}), bf16[8,16,2,16,512]{4,3,2,1,0:T(8,128)(2,1)}, u32[]{:S(2)}, u32[]{:S(2)}) async-start(bf16[8,16,2,16,512]{4,3,2,1,0:T(8,128)(2,1)} %stack.2), calls=%async_computation.2 | async-start | bytes 8388608 | tf_op jit(solution)/shard_map/all_to_all | solution.py:16
  68.6 0.7 multiply_bitcast_fusion
  69.2 0.1 add_multiply_fusion
  69.3 0.1 broadcast_compare_fusion
  69.4 0.1 lt.61
  69.5 0.9 reshape.313
  70.4 0.7 iota_compare_fusion.1
  71.1 0.1 fusion.39
  71.3 0.0 copy-done
  71.3 1.2 fusion.17
  72.5 0.4 fusion.40
  72.9 0.4 fusion.25
  73.3 0.2 convolution_bitcast_fusion
  73.5 44.8 %all-to-all-done.2 = bf16[8,16,2,16,512]{4,3,2,1,0:T(8,128)(2,1)} async-done(((bf16[8,16,2,16,512]{4,3,2,1,0:T(8,128)(2,1)}), bf16[8,16,2,16,512]{4,3,2,1,0:T(8,128)(2,1)}, u32[]{:S(2)}, u32[]{:S(2)}) %all-to-all-start.2) | async-done | bytes 4194336 | tf_op jit(solution)/shard_map/all_to_all | solution.py:16
  118.3 5.0 %copy.46 = bf16[16,8,2,16,512]{4,3,2,1,0:T(8,128)(2,1)} copy(bf16[16,8,2,16,512]{4,3,2,0,1:T(8,128)(2,1)} %bitcast.20) | data formatting | bytes 8388608 | tf_op jit(solution)/shard_map/reshape | solution.py:17
  123.3 6.9 %reshape_transpose_reshape_reshape.3 = bf16[1,4096,2,2,128]{4,3,2,1,0:T(2,128)(2,1)} reshape(bf16[16,8,2,16,512]{4,3,2,1,0:T(8,128)(2,1)} %copy.46) | data formatting | bytes 8388608 | tf_op jit(solution)/shard_map/reshape;transpose;reshape;reshape | solution.py:101
  130.2 8.9 %fusion.38 = (bf16[1,4096,2,1,128]{4,3,2,1,0:T(2,128)(2,1)S(1)}, bf16[1,4096,2,1,128]{4,3,2,1,0:T(2,128)(2,1)S(1)}) fusion(bf16[1,4096,2,2,128]{4,3,2,1,0:T(2,128)(2,1)} %reshape_transpose_reshape_reshape.3), kind=kLoop, calls=%fused_computation.56 | loop fusion | bytes 8388608 | tf_op jit(solution)/shard_map/slice | solution.py:113
  139.1 2.9 %fusion.1 = (f32[2,8,64]{1,2,0:T(8,128)S(1)}, f32[2,64,8,4096]{3,2,1,0:T(8,128)S(1)}) fusion(pred[4096]{0:T(1024)(128)(4,1)S(1)} %lt.61, bf16[1,4096,2,1,128]{4,3,2,1,0:T(2,128)(2,1)S(1)} %get-tuple-element.7, bf16[64,2,8,128]{3,2,1,0:T(8,128)(2,1)S(1)} %bitcast.144), kind=kOutput, calls=%fused_computation.3 | convolution fusion | flops 1086323712 | bytes 19144704 | tf_op jit(solution)/shard_map/bnkgd,blkd->bkgnl/dot_general | solution.py:110
  142.0 4.9 %fusion.2 = f32[2,8,64]{1,2,0:T(8,128)S(1)} fusion(f32[2,64,8,4096]{3,2,1,0:T(8,128)S(1)} %get-tuple-element.16, f32[2,8,64]{1,2,0:T(8,128)S(1)} %max.17, pred[4096]{0:T(1024)(128)(4,1)S(1)} %lt.61), kind=kLoop, calls=%fused_computation.4 | loop fusion | flops 20970496 | bytes 16789504 | tf_op jit(solution)/shard_map/reduce_sum | solution.py:122
  147.0 4.8 %fusion.21 = f32[1,64,2,8,128]{4,3,1,2,0:T(8,128)} fusion(bf16[1,4096,2,1,128]{4,3,2,1,0:T(2,128)(2,1)S(1)} %get-tuple-element.8, f32[2,64,8,4096]{3,2,1,0:T(8,128)S(1)} %get-tuple-element.16, f32[2,8,64]{1,2,0:T(8,128)S(1)} %max.17, pred[4096]{0:T(1024)(128)(4,1)S(1)} %lt.61, f32[2,8,64,128]{3,2,1,0:T(8,128)S(1)} %bitcast.147, ...), kind=kOutput, calls=%fused_computation.23 | convolution fusion | flops 1095106560 | bytes 19939328 | tf_op jit(solution)/shard_map/bkgnl,blkd->bkgnd/dot_general | solution.py:123
  151.7 1.1 copy.51
  152.8 0.5 fusion.24
  153.4 0.9 copy.52
  (10 shorter events, 0.2 us)
Async XLA Ops:
  0.0 71.3 %copy-start = (bf16[128,2048]{1,0:T(8,128)(2,1)S(1)}, bf16[128,2048]{1,0:T(8,128)(2,1)}, u32[]{:S(2)}) copy-start(bf16[128,2048]{1,0:T(8,128)(2,1)} %param.15) | copy-start | bytes 1572868
  64.0 54.3 %all-to-all-start.2 = ((bf16[8,16,2,16,512]{4,3,2,1,0:T(8,128)(2,1)}), bf16[8,16,2,16,512]{4,3,2,1,0:T(8,128)(2,1)}, u32[]{:S(2)}, u32[]{:S(2)}) async-start(bf16[8,16,2,16,512]{4,3,2,1,0:T(8,128)(2,1)} %stack.2), calls=%async_computation.2 | async-start | bytes 8388608 | tf_op jit(solution)/shard_map/all_to_all | solution.py:16
